TPU v7x, 32 devices: a whole 2x2x4 slice. The times are simulated.
32 devices in a mesh: parts: 2 (over x), tile: 16 (over z, y, core).
Axes of the slice: x: 2, y: 2, z: 4, core: 2. Of those that a mesh axis runs over, the one named last changes fastest.
Arguments:
- probe_wave: float32 [2, 128, 128], replicated, may hold values from -6 to 6
- object_slices: float32 [8, 2, 2048, 1024], P('parts', None, 'tile'), parts along dimension 0, may hold values from -4 to 4
- intensities: float32 [256, 128, 128], P(('parts', 'tile')), parts along dimension 0, may hold values from 0 to 2
- row_offset: int32 [256], P(('parts', 'tile')), parts along dimension 0, may hold values from 0 to 127
- col_offset: int32 [256], P(('parts', 'tile')), parts along dimension 0, may hold values from 0 to 896
- counts: int32 [32], P(('parts', 'tile')), parts along dimension 0, may hold values from 1 to 8, 64 in all
Outputs:
- object_grad: float32 [8, 2, 2048, 1024], P('parts', None, 'tile'), parts along dimension 0
- misfit_total: float32 [2], P('parts'), parts along dimension 0
There are 2 independent parts, one for each index of `parts`. A program takes and returns all parts, laid end to end along the dimension named above; an argument that names none is the same for every part. Nothing has to cross between parts.
Inputs may be any that keep to these rules, and one draw needn't show every extreme that they name: `counts`: every strip holds at least one position; some strip holds exactly 8.
All inputs are finite; a program needn't handle non-finite values. No bound on the sum of `counts` on one device may be relied on, other than what follows from the above.
Results may differ from a plain program's by a relative error of at most 0.0003.
Values sent between devices are 32-bit elements; how exact they have to be, the bound alone decides.
No kernel may reach another device: no remote copies, remote signals or barrier semaphores. Data moves between devices by JAX's collectives and lax.ppermute only.
A program may use at most 128 MiB of HBM per device.

v0:
```python
import functools

import jax
import jax.numpy as jnp
import ml_dtypes
import numpy as np
from jax import lax
from jax.experimental import pallas as pl
from jax.experimental.pallas import tpu as pltpu
from jax.sharding import PartitionSpec as P

BATCH = 2
UNIT = 8
ROW, COL, AT_PUSH, AT_BACK, AT_PULL, PUSHED, KEPT, TOTALS = range(8)


def make_tables(width):
    indices = np.arange(width)
    dft = np.exp(-2j * np.pi * (np.outer(indices, indices) % width) / width) / np.sqrt(width)
    freqs = np.where(indices < width // 2, indices, indices - width).astype(np.float64)
    along = np.conj(dft) @ (np.exp(-0.0015j * freqs**2)[:, None] * dft)
    out = []
    for matrix in (along, dft):
        left = np.block([[matrix.real, -matrix.imag], [matrix.imag, matrix.real]])
        forms = []
        for form in (left, left.T):
            form = form.astype(np.float32)
            high = form.astype(ml_dtypes.bfloat16)
            low = (form - high.astype(np.float32)).astype(ml_dtypes.bfloat16)
            forms.append(np.stack([high, low]))
        out.append(np.stack(forms))
    return np.stack(out)


def split(x):
    high = x.astype(jnp.bfloat16)
    return high, (x - high.astype(jnp.float32)).astype(jnp.bfloat16)


def dot(a, b):
    return jnp.dot(a, b, preferred_element_type=jnp.float32)


def two_sided(tables, which, conj, re, im):
    batch, width = len(re), re[0].shape[0]
    left_form, right_form = (1, 0) if conj else (0, 1)
    rows = jnp.concatenate([jnp.concatenate([a, b], axis=1) for a, b in zip(re, im)], axis=0)
    high, low = split(rows)
    m_high, m_low = tables[which, right_form, 0], tables[which, right_form, 1]
    out = dot(high, m_high) + (dot(high, m_low) + dot(low, m_high))
    re = [out[b * width : (b + 1) * width, :width] for b in range(batch)]
    im = [out[b * width : (b + 1) * width, width:] for b in range(batch)]
    cols = jnp.concatenate([jnp.concatenate(re, axis=1), jnp.concatenate(im, axis=1)], axis=0)
    high, low = split(cols)
    m_high, m_low = tables[which, left_form, 0], tables[which, left_form, 1]
    out = dot(m_high, high) + (dot(m_low, high) + dot(m_high, low))
    re = [out[:width, b * width : (b + 1) * width] for b in range(batch)]
    im = [out[width:, b * width : (b + 1) * width] for b in range(batch)]
    return re, im


def field_grads(tables, wave_ref, window_ref, measured, scales):
    batch, slices = wave_ref.shape[:2]
    for layer in range(slices):
        re, im = [], []
        for b in range(batch):
            w_re, w_im = wave_ref[b, layer, 0], wave_ref[b, layer, 1]
            t_re, t_im = window_ref[b, layer, 0], window_ref[b, layer, 1]
            re.append(w_re * t_re - w_im * t_im)
            im.append(w_re * t_im + w_im * t_re)
        if layer + 1 < slices:
            re, im = two_sided(tables, 0, False, re, im)
            for b in range(batch):
                wave_ref[b, layer + 1, 0] = re[b]
                wave_ref[b, layer + 1, 1] = im[b]
    re, im = two_sided(tables, 1, False, re, im)
    loss = 0.0
    back_re, back_im = [], []
    for b in range(batch):
        misfit = re[b] * re[b] + im[b] * im[b] - measured[b]
        loss = loss + scales[b] * (0.25 * jnp.sum(misfit * misfit))
        back_re.append(misfit * re[b])
        back_im.append(misfit * im[b])
    re, im = two_sided(tables, 1, True, back_re, back_im)
    for layer in reversed(range(slices)):
        upper_re, upper_im = [], []
        for b in range(batch):
            w_re, w_im = wave_ref[b, layer, 0], wave_ref[b, layer, 1]
            t_re, t_im = window_ref[b, layer, 0], window_ref[b, layer, 1]
            window_ref[b, layer, 0] = re[b] * w_re + im[b] * w_im
            window_ref[b, layer, 1] = im[b] * w_re - re[b] * w_im
            upper_re.append(re[b] * t_re + im[b] * t_im)
            upper_im.append(im[b] * t_re - re[b] * t_im)
        if layer > 0:
            re, im = two_sided(tables, 0, True, upper_re, upper_im)
    return loss


def place(plan_ref, slot, width, columns):
    row, col = plan_ref[ROW, slot], plan_ref[COL, slot]
    tile = col // width
    here = pl.ds(pl.multiple_of(tile * width, width), width)
    after = jnp.minimum(tile + 1, columns // width - 1)
    there = pl.ds(pl.multiple_of(after * width, width), width)
    return row, col - tile * width, here, there


def sizes(cap, width):
    whole = cap * width // UNIT
    return whole * 5 // 16, whole // 4, whole * 5 // 16


def make_plan(count_ref, row_ref, col_ref, plan_ref, width, room):
    cap = row_ref.shape[0]
    units = width // UNIT
    seen_units = width // (UNIT * UNIT)
    shape = (UNIT, 128)
    choice = lax.broadcasted_iota(jnp.int32, shape, 0) * 128 + lax.broadcasted_iota(jnp.int32, shape, 1)
    zero = jnp.zeros(shape, jnp.int32)
    push, back, pull, kept, bad = zero, zero, zero, zero, (choice >= (1 << cap)).astype(jnp.int32)
    count = count_ref[0]
    for s in range(cap):
        row = row_ref[s]
        crosses = jnp.logical_and(s < count, row > 0).astype(jnp.int32)
        taken = (choice >> s) & 1
        ahead = units - row // UNIT
        push += taken * (ahead + seen_units)
        back += taken * ahead
        pull += (1 - taken) * (crosses * ((row + UNIT - 1) // UNIT))
        kept += 1 - taken
        bad += taken * (1 - crosses)
    bad += (push > room[0]).astype(jnp.int32) + (back > room[1]).astype(jnp.int32) + (pull > room[2]).astype(jnp.int32)
    score = (kept + 16 * (bad > 0).astype(jnp.int32)) * (1 << cap) + choice
    best = jnp.min(score.astype(jnp.float32)).astype(jnp.int32)
    at_push = at_back = at_pull = n_pushed = n_kept = jnp.int32(0)
    for s in range(cap):
        plan_ref[PUSHED, s] = 0
        plan_ref[KEPT, s] = 0
        plan_ref[TOTALS, s] = 0
    for s in range(cap):
        row = row_ref[s]
        taken = (best >> s) & 1
        kept = jnp.where(s < count, 1 - taken, 0)
        plan_ref[ROW, s] = row
        plan_ref[COL, s] = col_ref[s]
        plan_ref[AT_PUSH, s] = at_push
        plan_ref[AT_BACK, s] = at_back
        plan_ref[AT_PULL, s] = at_pull

        @pl.when(taken > 0)
        def _():
            plan_ref[PUSHED, n_pushed] = s

        @pl.when(kept > 0)
        def _():
            plan_ref[KEPT, n_kept] = s

        ahead = units - row // UNIT
        at_push += taken * (ahead + seen_units)
        at_back += taken * ahead
        at_pull += kept * ((row + UNIT - 1) // UNIT)
        n_pushed += taken
        n_kept += kept
    plan_ref[TOTALS, 0] = n_pushed
    plan_ref[TOTALS, 1] = n_kept


def pack(plan_ref, slot, own_ref, buffer_ref, start, first_unit, last_unit):
    slices, planes, width, columns = own_ref.shape
    _, shift, here, there = place(plan_ref, slot, width, columns)
    first = lax.broadcasted_iota(jnp.int32, (UNIT, width), 1) >= shift

    def step(u, carry):
        rows = pl.ds(pl.multiple_of(u * UNIT, UNIT), UNIT)
        for l in range(slices):
            for p in range(planes):
                buffer_ref[start + u - first_unit, l * planes + p] = jnp.where(
                    first, own_ref[l, p, rows, here], own_ref[l, p, rows, there]
                )
        return carry

    lax.fori_loop(first_unit, last_unit, step, 0)


def push_kernel(count_ref, row_ref, col_ref, own_hbm, seen_hbm, plan_ref, out_hbm, own_ref, buffer_ref, sem, seen_sem, *, room):
    width = own_ref.shape[2]
    units, seen_units = width // UNIT, seen_hbm.shape[1]
    load = pltpu.make_async_copy(own_hbm, own_ref, sem)
    load.start()
    make_plan(count_ref, row_ref, col_ref, plan_ref, width, room)
    load.wait()

    def step(i, carry):
        slot = plan_ref[PUSHED, i]
        start, low = plan_ref[AT_PUSH, slot], plan_ref[ROW, slot] // UNIT
        seen = pltpu.make_async_copy(
            seen_hbm.at[slot], buffer_ref.at[pl.ds(start + units - low, seen_units)], seen_sem
        )
        seen.start()
        pack(plan_ref, slot, own_ref, buffer_ref, start, low, units)
        seen.wait()
        return carry

    lax.fori_loop(0, plan_ref[TOTALS, 0], step, 0)
    store = pltpu.make_async_copy(buffer_ref, out_hbm, sem)
    store.start()
    store.wait()


def pull_kernel(plan_ref, own_hbm, out_hbm, own_ref, buffer_ref, sem):
    load = pltpu.make_async_copy(own_hbm, own_ref, sem)
    load.start()
    load.wait()

    def step(i, carry):
        slot = plan_ref[KEPT, i]
        pack(plan_ref, slot, own_ref, buffer_ref, plan_ref[AT_PULL, slot], 0, (plan_ref[ROW, slot] + UNIT - 1) // UNIT)
        return carry

    lax.fori_loop(0, plan_ref[TOTALS, 1], step, 0)
    store = pltpu.make_async_copy(buffer_ref, out_hbm, sem)
    store.start()
    store.wait()


def grad_kernel(plan_ref, loss_in_ref, probe_hbm, own_hbm, came_hbm, seen_hbm, tables_hbm, grad_in_hbm,
                grad_hbm, back_hbm, loss_ref,
                probe_ref, own_ref, came_ref, seen_ref, tables_ref, grad_ref, back_ref, wave_ref, window_ref, sems,
                *, pushed):
    slices, planes, width, columns = own_ref.shape
    units = width // UNIT
    seen_units = width // (UNIT * UNIT)
    came = pl.ds(units, came_hbm.shape[0])
    loads = [
        pltpu.make_async_copy(probe_hbm, probe_ref, sems.at[0]),
        pltpu.make_async_copy(own_hbm, own_ref, sems.at[1]),
        pltpu.make_async_copy(came_hbm, came_ref.at[came], sems.at[2]),
        pltpu.make_async_copy(tables_hbm, tables_ref, sems.at[3]),
    ]
    if not pushed:
        loads.append(pltpu.make_async_copy(seen_hbm, seen_ref, sems.at[4]))
        loads.append(pltpu.make_async_copy(grad_in_hbm, grad_ref, sems.at[5]))
    for load in loads:
        load.start()
    if pushed:
        grad_ref[...] = jnp.zeros_like(grad_ref)
    for load in loads:
        load.wait()
    row_iota = lax.broadcasted_iota(jnp.int32, (width, width), 0)
    lane_iota = lax.broadcasted_iota(jnp.int32, (width, width), 1)
    count = plan_ref[TOTALS, 0 if pushed else 1]

    def step(group, loss):
        slots, scales, measured = [], [], []
        for b in range(BATCH):
            live = group * BATCH + b < count
            slot = plan_ref[PUSHED if pushed else KEPT, jnp.where(live, group * BATCH + b, group * BATCH)]
            slots.append(slot)
            scales.append(live.astype(jnp.float32))
            row, shift, here, there = place(plan_ref, slot, width, columns)
            mine = row_iota < row if pushed else row_iota >= row
            first = lane_iota >= shift
            low = row // UNIT
            if pushed:
                start = units + plan_ref[AT_PUSH, slot] - low
                seen = came_ref[pl.ds(start + units, seen_units)]
                measured.append(seen.reshape(width, width))
            else:
                start = units + plan_ref[AT_PULL, slot]
                measured.append(seen_ref[slot])
            for l in range(slices):
                for p in range(planes):
                    theirs = came_ref[pl.ds(start, units), l * planes + p].reshape(width, width)
                    ours = jnp.where(first, own_ref[l, p, :, here], own_ref[l, p, :, there])
                    window_ref[b, l, p] = jnp.where(mine, ours, theirs)
            for p in range(planes):
                wave_ref[b, 0, p] = pltpu.roll(pltpu.roll(probe_ref[p], row, 0), shift, 1)
        loss = loss + field_grads(tables_ref, wave_ref, window_ref, measured, scales)
        for b in range(BATCH):
            row, shift, here, there = place(plan_ref, slots[b], width, columns)
            mine = row_iota < row if pushed else row_iota >= row
            first = lane_iota >= shift
            if pushed:
                start, begin, end = plan_ref[AT_BACK, slots[b]], row // UNIT, units
            else:
                start, begin, end = plan_ref[AT_PULL, slots[b]], 0, (row + UNIT - 1) // UNIT

            @pl.when(scales[b] > 0)
            def _(b=b, mine=mine, first=first, here=here, there=there, start=start, begin=begin, end=end):
                for l in range(slices):
                    for p in range(planes):
                        ours = jnp.where(mine, window_ref[b, l, p], 0.0)
                        grad_ref[l, p, :, here] += jnp.where(first, ours, 0.0)
                        grad_ref[l, p, :, there] += jnp.where(first, 0.0, ours)

                def unit(u, carry):
                    rows = pl.ds(pl.multiple_of(u * UNIT, UNIT), UNIT)
                    for l in range(slices):
                        for p in range(planes):
                            back_ref[start + u - begin, l * planes + p] = window_ref[b, l, p, rows, :]
                    return carry

                lax.fori_loop(begin, end, unit, 0)

        return loss

    loss_ref[0] = lax.fori_loop(0, (count + BATCH - 1) // BATCH, step, loss_in_ref[0])
    stores = [
        pltpu.make_async_copy(grad_ref, grad_hbm, sems.at[0]),
        pltpu.make_async_copy(back_ref, back_hbm, sems.at[1]),
    ]
    for store in stores:
        store.start()
    for store in stores:
        store.wait()


def add_kernel(plan_ref, before_ref, grad_in_hbm, pushed_hbm, pulled_hbm, grad_hbm,
               grad_ref, pushed_ref, pulled_ref, sems):
    slices, planes, width, columns = grad_ref.shape
    units = width // UNIT
    loads = [pltpu.make_async_copy(grad_in_hbm.at[l], grad_ref.at[l], sems.at[l]) for l in range(slices)]
    stores = [pltpu.make_async_copy(grad_ref.at[l], grad_hbm.at[l], sems.at[slices + l]) for l in range(slices)]
    others = [
        pltpu.make_async_copy(pushed_hbm, pushed_ref, sems.at[2 * slices]),
        pltpu.make_async_copy(pulled_hbm, pulled_ref, sems.at[2 * slices + 1]),
    ]
    for load in others + loads:
        load.start()
    for load in others:
        load.wait()
    lane_iota = lax.broadcasted_iota(jnp.int32, (UNIT, width), 1)
    row_iota = lax.broadcasted_iota(jnp.int32, (UNIT, width), 0)

    def add(plan, slot, l, came, start, begin, end, below):
        row, shift, here, there = place(plan, slot, width, columns)
        first = lane_iota >= shift

        def unit(u, carry):
            rows = pl.ds(pl.multiple_of(u * UNIT, UNIT), UNIT)
            at = u * UNIT + row_iota
            mine = at < row if below else at >= row
            for p in range(planes):
                piece = jnp.where(mine, came[start + u - begin, l * planes + p], 0.0)
                grad_ref[l, p, rows, here] += jnp.where(first, piece, 0.0)
                grad_ref[l, p, rows, there] += jnp.where(first, 0.0, piece)
            return carry

        lax.fori_loop(begin, end, unit, 0)

    for l in range(slices):
        loads[l].wait()

        def returned(i, carry, l=l):
            slot = plan_ref[PUSHED, i]
            add(plan_ref, slot, l, pushed_ref, plan_ref[AT_BACK, slot], plan_ref[ROW, slot] // UNIT, units, False)
            return carry

        def given(i, carry, l=l):
            slot = before_ref[KEPT, i]
            end = (before_ref[ROW, slot] + UNIT - 1) // UNIT
            add(before_ref, slot, l, pulled_ref, before_ref[AT_PULL, slot], 0, end, True)
            return carry

        lax.fori_loop(0, plan_ref[TOTALS, 0], returned, 0)
        lax.fori_loop(0, before_ref[TOTALS, 1], given, 0)
        stores[l].start()
    for store in stores:
        store.wait()


def shifted(x, axis, by):
    peers = lax.axis_size(axis)
    return lax.ppermute(x, axis, [(i, (i + by) % peers) for i in range(peers)])


def total_of(x, axis):
    peers = lax.axis_size(axis)
    step = 1
    while step < peers:
        def other(by):
            return lax.ppermute(x, axis, [(i, i ^ by) for i in range(peers)])

        if step * 4 <= peers:
            x = (x + other(step)) + (other(2 * step) + other(3 * step))
            step *= 4
        else:
            x = x + other(step)
            step *= 2
    return x


def local(probe_wave, object_slices, intensities, row_offset, col_offset, counts):
    width = probe_wave.shape[-1]
    slices, planes = object_slices.shape[:2]
    cap = row_offset.shape[0]
    units = width // UNIT
    seen_units = width // (UNIT * UNIT)
    tables = jnp.asarray(make_tables(width))
    seen = intensities.reshape(cap, seen_units, UNIT, UNIT, width)
    room = sizes(cap, width)
    smem = pl.BlockSpec(memory_space=pltpu.SMEM)
    hbm = pl.BlockSpec(memory_space=pl.ANY)
    f32 = jnp.float32

    def packed(n):
        return (n, slices * planes, UNIT, width)

    def shape(dims, dtype=f32):
        return jax.ShapeDtypeStruct(dims, dtype)

    params = pltpu.CompilerParams(vmem_limit_bytes=48 << 20)
    strip = object_slices.shape
    plan, push = pl.pallas_call(
        functools.partial(push_kernel, room=room),
        out_shape=(shape((8, cap), jnp.int32), shape(packed(room[0]))),
        in_specs=[smem] * 3 + [hbm] * 2,
        out_specs=(smem, hbm),
        scratch_shapes=[
            pltpu.VMEM(strip, f32),
            pltpu.VMEM(packed(room[0]), f32),
            pltpu.SemaphoreType.DMA,
            pltpu.SemaphoreType.DMA,
        ],
        compiler_params=params,
        name="pack_pushed",
    )(counts, row_offset, col_offset, object_slices, seen)
    pushed = shifted(push, "tile", 1)
    before = shifted(plan, "tile", 1)
    pull = pl.pallas_call(
        pull_kernel,
        out_shape=shape(packed(room[2])),
        in_specs=[smem, hbm],
        out_specs=hbm,
        scratch_shapes=[
            pltpu.VMEM(strip, f32),
            pltpu.VMEM(packed(room[2]), f32),
            pltpu.SemaphoreType.DMA,
        ],
        compiler_params=params,
        name="pack_pulled",
    )(before, object_slices)
    pulled = shifted(pull, "tile", -1)

    def grads(plan, loss, came, grad, back, is_pushed):
        return pl.pallas_call(
            functools.partial(grad_kernel, pushed=is_pushed),
            out_shape=(shape(strip), shape(packed(back)), shape((1,))),
            in_specs=[smem, smem] + [hbm] * 6,
            out_specs=(hbm, hbm, smem),
            scratch_shapes=[
                pltpu.VMEM(probe_wave.shape, f32),
                pltpu.VMEM(strip, f32),
                pltpu.VMEM(packed(came.shape[0] + 2 * units), f32),
                pltpu.VMEM(intensities.shape, f32),
                pltpu.VMEM(tables.shape, tables.dtype),
                pltpu.VMEM(strip, f32),
                pltpu.VMEM(packed(back), f32),
                pltpu.VMEM((BATCH, slices, planes, width, width), f32),
                pltpu.VMEM((BATCH, slices, planes, width, width), f32),
                pltpu.SemaphoreType.DMA((6,)),
            ],
            compiler_params=params,
            name="grads_pushed" if is_pushed else "grads_kept",
        )(plan, loss, probe_wave, object_slices, came, intensities, tables, grad)

    grad, back, loss = grads(before, jnp.zeros((1,), f32), pushed, object_slices, room[1], True)
    returned = shifted(back, "tile", -1)
    grad, back, loss = grads(plan, loss, pulled, grad, room[2], False)
    given = shifted(back, "tile", 1)
    misfit_total = total_of(loss, "tile")
    grad = pl.pallas_call(
        add_kernel,
        out_shape=shape(strip),
        in_specs=[smem, smem] + [hbm] * 3,
        out_specs=hbm,
        scratch_shapes=[
            pltpu.VMEM(strip, f32),
            pltpu.VMEM(packed(room[1]), f32),
            pltpu.VMEM(packed(room[2]), f32),
            pltpu.SemaphoreType.DMA((2 * slices + 2,)),
        ],
        compiler_params=params,
        name="add_returned",
    )(plan, before, grad, returned, given)
    return (grad, misfit_total)


def solution(mesh):
    placed = (
        P(),
        P("parts", None, "tile", None),
        P(("parts", "tile"), None, None),
        P(("parts", "tile")),
        P(("parts", "tile")),
        P(("parts", "tile")),
    )
    return jax.shard_map(
        local,
        mesh=mesh,
        in_specs=placed,
        out_specs=(P("parts", None, "tile", None), P("parts")),
        check_vma=False,
    )
```

profile of v0, /device:TPU:14, one launch (start us, length us, event | category | flops | bytes accessed | tf_op | source)
XLA Modules:
  0.0 120.8 jit_solution(4457376020411844771)
XLA Ops:
  1.3 0.0 copy-start
  1.3 2.2 %copy-done = f32[4,2,128,1024]{3,2,1,0:T(8,128)S(1)} copy-done((f32[4,2,128,1024]{3,2,1,0:T(8,128)S(1)}, f32[4,2,128,1024]{3,2,1,0:T(8,128)}, u32[]{:S(2)}) %copy-start) | copy-done | bytes 4194328
  3.5 1.0 copy-done.2
  4.5 0.7 copy-done.6
  5.2 0.7 copy-done.7
  5.8 2.6 %pack_pushed.1 = (s32[8,8]{1,0:T(8,128)S(1)}, f32[40,8,8,128]{3,2,1,0:T(8,128)S(1)}) custom-call(s32[1]{0:T(128)S(6)} %copy.9.count_ref, s32[8]{0:T(128)S(1)} %copy-done.6, s32[8]{0:T(128)S(1)} %copy-done.7, f32[4,2,128,1024]{3,2,1,0:T(8,128)S(1)} %copy-done, f32[8,2,8,8,128]{4,3,2,1,0:T(8,128)S(1)} %bitcast.1), custom_call_target="tpu_custom_call" | custom-call | tf_op jit(solution)/shard_map/pack_pushed/pallas_call | solution.py:414
  8.4 0.1 collective-permute-start
  8.5 0.0 copy-start.3
  8.5 0.0 copy-start.4
  8.5 0.0 copy-start.5
  8.5 1.4 %collective-permute-start.1 = (f32[40,8,8,128]{3,2,1,0:T(8,128)S(1)}, f32[40,8,8,128]{3,2,1,0:T(8,128)S(1)}, u32[]{:S(2)}, u32[]{:S(2)}) collective-permute-start(f32[40,8,8,128]{3,2,1,0:T(8,128)S(1)} %get-tuple-element.11), channel_id=1, source_target_pairs={{0,1},{1,2},{2,3},{3,4},{4,5},{5,6},{6,7},{7,8},{8,9},{9,10},{10,1... | collective-permute-start | bytes 3932168 | tf_op jit(solution)/shard_map/ppermute | solution.py:374
  9.9 1.6 %collective-permute-done.plan_ref.before_ref = s32[8,8]{1,0:T(8,128)S(1)} collective-permute-done((s32[8,8]{1,0:T(8,128)S(1)}, s32[8,8]{1,0:T(8,128)S(1)}, u32[]{:S(2)}, u32[]{:S(2)}) %collective-permute-start) | collective-permute-done | bytes 288 | tf_op jit(solution)/shard_map/ppermute | solution.py:374
  11.5 1.2 %pack_pulled.1 = f32[40,8,8,128]{3,2,1,0:T(8,128)S(1)} custom-call(s32[8,8]{1,0:T(8,128)S(1)} %collective-permute-done.plan_ref.before_ref, f32[4,2,128,1024]{3,2,1,0:T(8,128)S(1)} %copy-done.1), custom_call_target="tpu_custom_call" | custom-call | tf_op jit(solution)/shard_map/pack_pulled/pallas_call | solution.py:430
  12.7 0.1 collective-permute-start.2
  12.8 26.9 %collective-permute-done.1.came_hbm = f32[40,8,8,128]{3,2,1,0:T(8,128)S(1)} collective-permute-done((f32[40,8,8,128]{3,2,1,0:T(8,128)S(1)}, f32[40,8,8,128]{3,2,1,0:T(8,128)S(1)}, u32[]{:S(2)}, u32[]{:S(2)}) %collective-permute-start.1) | collective-permute-done | bytes 1310752 | tf_op jit(solution)/shard_map/ppermute | solution.py:374
  39.6 22.9 %grads_pushed.1 = (f32[4,2,128,1024]{3,2,1,0:T(8,128)}, f32[32,8,8,128]{3,2,1,0:T(8,128)S(1)}, f32[1]{0:T(128)}) custom-call(s32[8,8]{1,0:T(8,128)S(1)} %collective-permute-done.plan_ref.before_ref, f32[1]{0:T(128)} %constant.1.clone.1.loss_in_ref, f32[2,128,128]{2,1,0:T(8,128)S(1)} %copy-done.5, f32[4,2,128,1024]{3,2,1,0:T(8,128)} %own_hbm.7, ...), custom_call_target="tpu_custom_call" | custom-call | tf_op jit(solution)/shard_map/grads_pushed/pallas_call | solution.py:446
  62.6 0.0 collective-permute-done.2.came_hbm
  62.6 19.1 %grads_kept.1 = (f32[4,2,128,1024]{3,2,1,0:T(8,128)}, f32[40,8,8,128]{3,2,1,0:T(8,128)S(1)}, f32[1]{0:T(128)}) custom-call(s32[8,8]{1,0:T(8,128)S(1)} %get-tuple-element.10.plan_ref, f32[1]{0:T(128)} %get-tuple-element.12.loss_in_ref, f32[2,128,128]{2,1,0:T(8,128)S(1)} %copy-done.5, f32[4,2,128,1024]{3,2,1,0:T(8,128)} %own_hbm.7, ...), custom_call_target="tpu_custom_call" | custom-call | tf_op jit(solution)/shard_map/grads_kept/pallas_call | solution.py:446
  81.7 0.1 collective-permute-start.4
  81.8 1.7 %collective-permute-start.3 = (f32[32,8,8,128]{3,2,1,0:T(8,128)S(1)}, f32[32,8,8,128]{3,2,1,0:T(8,128)S(1)}, u32[]{:S(2)}, u32[]{:S(2)}) collective-permute-start(f32[32,8,8,128]{3,2,1,0:T(8,128)S(1)} %get-tuple-element.15), channel_id=1, source_target_pairs={{0,15},{1,0},{2,1},{3,2},{4,3},{5,4},{6,5},{7,6},{8,7},{9,8},{10,9... | collective-permute-start | bytes 3145736 | tf_op jit(solution)/shard_map/ppermute | solution.py:374
  83.5 0.0 collective-permute-start.7
  83.5 0.4 collective-permute-start.6
  84.0 1.4 %collective-permute-start.5 = (f32[1]{0:T(128)}, f32[1]{0:T(128)}, u32[]{:S(2)}, u32[]{:S(2)}) collective-permute-start(f32[1]{0:T(128)} %get-tuple-element.17), channel_id=1, source_target_pairs={{0,1},{1,0},{2,3},{3,2},{4,5},{5,4},{6,7},{7,6},{8,9},{9,8},{10,11... | collective-permute-start | bytes 20 | tf_op jit(solution)/shard_map/ppermute | solution.py:382
  85.4 0.9 collective-permute-done.5
  87.6 11.4 %collective-permute-done.7 = f32[1]{0:T(128)} collective-permute-done((f32[1]{0:T(128)}, f32[1]{0:T(128)}, u32[]{:S(2)}, u32[]{:S(2)}) %collective-permute-start.7) | collective-permute-done | bytes 36 | tf_op jit(solution)/shard_map/ppermute | solution.py:382
  99.0 0.0 collective-permute-done.6
  100.2 1.4 %collective-permute-start.10 = (f32[1]{0:T(128)}, f32[1]{0:T(128)}, u32[]{:S(2)}, u32[]{:S(2)}) collective-permute-start(f32[1]{0:T(128)} %add.20), channel_id=1, source_target_pairs={{0,12},{1,13},{2,14},{3,15},{4,8},{5,9},{6,10},{7,11},{8,4},{9,5},... | collective-permute-start | bytes 20 | tf_op jit(solution)/shard_map/ppermute | solution.py:382
  101.6 6.9 %collective-permute-start.9 = (f32[1]{0:T(128)}, f32[1]{0:T(128)}, u32[]{:S(2)}, u32[]{:S(2)}) collective-permute-start(f32[1]{0:T(128)} %add.20), channel_id=1, source_target_pairs={{0,8},{1,9},{2,10},{3,11},{4,12},{5,13},{6,14},{7,15},{8,0},{9,1},... | collective-permute-start | bytes 20 | tf_op jit(solution)/shard_map/ppermute | solution.py:382
  108.5 1.3 %collective-permute-start.8 = (f32[1]{0:T(128)}, f32[1]{0:T(128)}, u32[]{:S(2)}, u32[]{:S(2)}) collective-permute-start(f32[1]{0:T(128)} %add.20), channel_id=1, source_target_pairs={{0,4},{1,5},{2,6},{3,7},{4,0},{5,1},{6,2},{7,3},{8,12},{9,13},{10,... | collective-permute-start | bytes 20 | tf_op jit(solution)/shard_map/ppermute | solution.py:382
  109.8 2.3 %collective-permute-done.8 = f32[1]{0:T(128)} collective-permute-done((f32[1]{0:T(128)}, f32[1]{0:T(128)}, u32[]{:S(2)}, u32[]{:S(2)}) %collective-permute-start.8) | collective-permute-done | bytes 36 | tf_op jit(solution)/shard_map/ppermute | solution.py:382
  114.1 0.0 collective-permute-done.4.pulled_hbm
  114.1 5.6 %add_returned.1 = f32[4,2,128,1024]{3,2,1,0:T(8,128)} custom-call(s32[8,8]{1,0:T(8,128)S(1)} %get-tuple-element.10.plan_ref, s32[8,8]{1,0:T(8,128)S(1)} %collective-permute-done.plan_ref.before_ref, f32[4,2,128,1024]{3,2,1,0:T(8,128)} %get-tuple-element.14.grad_in_hbm, f32[32,8,8,128]{3,2,1,0:T(8,128)S(1)} %collective-permute-done.3.pushed_hbm, ...), custom_call_target="tpu_custom_call" | custom-call | tf_op jit(solution)/shard_map/add_returned/pallas_call | solution.py:472
  (11 shorter events, 0.0 us)
Async XLA Ops:
  1.3 2.2 %copy-start = (f32[4,2,128,1024]{3,2,1,0:T(8,128)S(1)}, f32[4,2,128,1024]{3,2,1,0:T(8,128)}, u32[]{:S(2)}) copy-start(f32[4,2,128,1024]{3,2,1,0:T(8,128)} %own_hbm.7) | copy-start | bytes 12582916
  3.5 1.0 copy-start.2
  4.5 0.7 copy-start.6
  5.2 0.7 copy-start.7
  5.8 5.7 %copy-start.1 = (f32[4,2,128,1024]{3,2,1,0:T(8,128)S(1)}, f32[4,2,128,1024]{3,2,1,0:T(8,128)}, u32[]{:S(2)}) copy-start(f32[4,2,128,1024]{3,2,1,0:T(8,128)} %own_hbm.7) | copy-start | bytes 12582916
  8.4 3.1 %collective-permute-start = (s32[8,8]{1,0:T(8,128)S(1)}, s32[8,8]{1,0:T(8,128)S(1)}, u32[]{:S(2)}, u32[]{:S(2)}) collective-permute-start(s32[8,8]{1,0:T(8,128)S(1)} %get-tuple-element.10.plan_ref), channel_id=1, source_target_pairs={{0,1},{1,2},{2,3},{3,4},{4,5},{5,6},{6,7},{7,8},{8,9},{9,10},{10,1... | collective-permute-start | bytes 776 | tf_op jit(solution)/shard_map/ppermute | solution.py:374
  8.5 31.2 %copy-start.3 = (f32[8,128,128]{2,1,0:T(8,128)S(1)}, f32[8,128,128]{2,1,0:T(8,128)}, u32[]{:S(2)}) copy-start(f32[8,128,128]{2,1,0:T(8,128)} %seen_hbm.3) | copy-start | bytes 1572868
  8.5 31.2 %copy-start.4 = (bf16[2,2,2,256,256]{4,3,2,1,0:T(8,128)(2,1)S(1)}, bf16[2,2,2,256,256]{4,3,2,1,0:T(8,128)(2,1)}, u32[]{:S(2)}) copy-start(bf16[2,2,2,256,256]{4,3,2,1,0:T(8,128)(2,1)} %constant.4.clone.tables_hbm) | copy-start | bytes 3145732
  8.5 31.1 %copy-start.5 = (f32[2,128,128]{2,1,0:T(8,128)S(1)}, f32[2,128,128]{2,1,0:T(8,128)}, u32[]{:S(2)}) copy-start(f32[2,128,128]{2,1,0:T(8,128)} %probe_hbm.3) | copy-start | bytes 393220
  8.5 31.1 %collective-permute-start.1 = (f32[40,8,8,128]{3,2,1,0:T(8,128)S(1)}, f32[40,8,8,128]{3,2,1,0:T(8,128)S(1)}, u32[]{:S(2)}, u32[]{:S(2)}) collective-permute-start(f32[40,8,8,128]{3,2,1,0:T(8,128)S(1)} %get-tuple-element.11), channel_id=1, source_target_pairs={{0,1},{1,2},{2,3},{3,4},{4,5},{5,6},{6,7},{7,8},{8,9},{9,10},{10,1... | collective-permute-start | bytes 3932168 | tf_op jit(solution)/shard_map/ppermute | solution.py:374
  12.7 49.9 %collective-permute-start.2 = (f32[40,8,8,128]{3,2,1,0:T(8,128)S(1)}, f32[40,8,8,128]{3,2,1,0:T(8,128)S(1)}, u32[]{:S(2)}, u32[]{:S(2)}) collective-permute-start(f32[40,8,8,128]{3,2,1,0:T(8,128)S(1)} %pack_pulled.1), channel_id=1, source_target_pairs={{0,15},{1,0},{2,1},{3,2},{4,3},{5,4},{6,5},{7,6},{8,7},{9,8},{10,9... | collective-permute-start | bytes 3932168 | tf_op jit(solution)/shard_map/ppermute | solution.py:374
  81.7 32.4 %collective-permute-start.4 = (f32[40,8,8,128]{3,2,1,0:T(8,128)S(1)}, f32[40,8,8,128]{3,2,1,0:T(8,128)S(1)}, u32[]{:S(2)}, u32[]{:S(2)}) collective-permute-start(f32[40,8,8,128]{3,2,1,0:T(8,128)S(1)} %get-tuple-element.16), channel_id=1, source_target_pairs={{0,1},{1,2},{2,3},{3,4},{4,5},{5,6},{6,7},{7,8},{8,9},{9,10},{10,1... | collective-permute-start | bytes 3932168 | tf_op jit(solution)/shard_map/ppermute | solution.py:374
  81.8 32.3 %collective-permute-start.3 = (f32[32,8,8,128]{3,2,1,0:T(8,128)S(1)}, f32[32,8,8,128]{3,2,1,0:T(8,128)S(1)}, u32[]{:S(2)}, u32[]{:S(2)}) collective-permute-start(f32[32,8,8,128]{3,2,1,0:T(8,128)S(1)} %get-tuple-element.15), channel_id=1, source_target_pairs={{0,15},{1,0},{2,1},{3,2},{4,3},{5,4},{6,5},{7,6},{8,7},{9,8},{10,9... | collective-permute-start | bytes 3145736 | tf_op jit(solution)/shard_map/ppermute | solution.py:374
  83.5 15.5 %collective-permute-start.7 = (f32[1]{0:T(128)}, f32[1]{0:T(128)}, u32[]{:S(2)}, u32[]{:S(2)}) collective-permute-start(f32[1]{0:T(128)} %get-tuple-element.17), channel_id=1, source_target_pairs={{0,3},{1,2},{2,1},{3,0},{4,7},{5,6},{6,5},{7,4},{8,11},{9,10},{10,... | collective-permute-start | bytes 20 | tf_op jit(solution)/shard_map/ppermute | solution.py:382
  83.5 15.4 %collective-permute-start.6 = (f32[1]{0:T(128)}, f32[1]{0:T(128)}, u32[]{:S(2)}, u32[]{:S(2)}) collective-permute-start(f32[1]{0:T(128)} %get-tuple-element.17), channel_id=1, source_target_pairs={{0,2},{1,3},{2,0},{3,1},{4,6},{5,7},{6,4},{7,5},{8,10},{9,11},{10,... | collective-permute-start | bytes 20 | tf_op jit(solution)/shard_map/ppermute | solution.py:382
  84.0 2.3 %collective-permute-start.5 = (f32[1]{0:T(128)}, f32[1]{0:T(128)}, u32[]{:S(2)}, u32[]{:S(2)}) collective-permute-start(f32[1]{0:T(128)} %get-tuple-element.17), channel_id=1, source_target_pairs={{0,1},{1,0},{2,3},{3,2},{4,5},{5,4},{6,7},{7,6},{8,9},{9,8},{10,11... | collective-permute-start | bytes 20 | tf_op jit(solution)/shard_map/ppermute | solution.py:382
  100.2 12.4 %collective-permute-start.10 = (f32[1]{0:T(128)}, f32[1]{0:T(128)}, u32[]{:S(2)}, u32[]{:S(2)}) collective-permute-start(f32[1]{0:T(128)} %add.20), channel_id=1, source_target_pairs={{0,12},{1,13},{2,14},{3,15},{4,8},{5,9},{6,10},{7,11},{8,4},{9,5},... | collective-permute-start | bytes 20 | tf_op jit(solution)/shard_map/ppermute | solution.py:382
  101.6 11.1 %collective-permute-start.9 = (f32[1]{0:T(128)}, f32[1]{0:T(128)}, u32[]{:S(2)}, u32[]{:S(2)}) collective-permute-start(f32[1]{0:T(128)} %add.20), channel_id=1, source_target_pairs={{0,8},{1,9},{2,10},{3,11},{4,12},{5,13},{6,14},{7,15},{8,0},{9,1},... | collective-permute-start | bytes 20 | tf_op jit(solution)/shard_map/ppermute | solution.py:382
  108.5 3.6 %collective-permute-start.8 = (f32[1]{0:T(128)}, f32[1]{0:T(128)}, u32[]{:S(2)}, u32[]{:S(2)}) collective-permute-start(f32[1]{0:T(128)} %add.20), channel_id=1, source_target_pairs={{0,4},{1,5},{2,6},{3,7},{4,0},{5,1},{6,2},{7,3},{8,12},{9,13},{10,... | collective-permute-start | bytes 20 | tf_op jit(solution)/shard_map/ppermute | solution.py:382
where the time goes:
time: 120 us; the launch traced here: 121 us
  Pallas kernels  51.4 us (43%)
  waiting for transfers between devices  43.1 us (36%)
  starting transfers between devices  14.6 us (12%)
  between operations  7.09 us (6%)
  local copies, waits for them, and re-layouts  4.56 us (4%)
    pallas_call x2, Pallas kernels, grads(): pl.pallas_call(functools.partial(grad_kernel, pushed=is_pushed), out_shap...  42 us
    ppermute x5, waiting for transfers between devices, shifted(): return lax.ppermute(x, axis, [(i, (i + by) % peers) for i in range(peers)])  28.5 us
    ppermute x6, waiting for transfers between devices, other(): return lax.ppermute(x, axis, [(i, i ^ by) for i in range(peers)])  14.6 us
    ppermute x6, starting transfers between devices, other(): return lax.ppermute(x, axis, [(i, i ^ by) for i in range(peers)])  11.4 us
    pallas_call x1, Pallas kernels, local(): pl.pallas_call(add_kernel, out_shape=shape(strip), in_specs=[smem, smem]...  5.57 us
    unnamed x16, local copies, waits for them, and re-layouts  4.56 us
    ppermute x5, starting transfers between devices, shifted(): return lax.ppermute(x, axis, [(i, (i + by) % peers) for i in range(peers)])  3.26 us
    pallas_call x1, Pallas kernels, local(): pl.pallas_call(functools.partial(push_kernel, room=room), out_shape=(shap...  2.57 us
  transfers between devices with their start and end apart: 11, of which 5 were waited for; matrix products, arithmetic and copies ran while one was open for 0% of the time, Pallas kernels for 20%

commit v1 on v0

--- a/solution.py
+++ b/solution.py
@@ -9,7 +9,7 @@
 from jax.experimental.pallas import tpu as pltpu
 from jax.sharding import PartitionSpec as P
 
-BATCH = 2
+BATCH = 4
 UNIT = 8
 ROW, COL, AT_PUSH, AT_BACK, AT_PULL, PUSHED, KEPT, TOTALS = range(8)
 
@@ -41,22 +41,19 @@
     return jnp.dot(a, b, preferred_element_type=jnp.float32)
 
 
+def one_sided(tables, which, form, re, im):
+    width = re.shape[0]
+    high, low = split(jnp.concatenate([re, im], axis=1))
+    m_high, m_low = tables[which, form, 0], tables[which, form, 1]
+    out = dot(high, m_high) + (dot(high, m_low) + dot(low, m_high))
+    return out[:, :width], out[:, width:]
+
+
 def two_sided(tables, which, conj, re, im):
-    batch, width = len(re), re[0].shape[0]
-    left_form, right_form = (1, 0) if conj else (0, 1)
-    rows = jnp.concatenate([jnp.concatenate([a, b], axis=1) for a, b in zip(re, im)], axis=0)
-    high, low = split(rows)
-    m_high, m_low = tables[which, right_form, 0], tables[which, right_form, 1]
-    out = dot(high, m_high) + (dot(high, m_low) + dot(low, m_high))
-    re = [out[b * width : (b + 1) * width, :width] for b in range(batch)]
-    im = [out[b * width : (b + 1) * width, width:] for b in range(batch)]
-    cols = jnp.concatenate([jnp.concatenate(re, axis=1), jnp.concatenate(im, axis=1)], axis=0)
-    high, low = split(cols)
-    m_high, m_low = tables[which, left_form, 0], tables[which, left_form, 1]
-    out = dot(m_high, high) + (dot(m_low, high) + dot(m_high, low))
-    re = [out[:width, b * width : (b + 1) * width] for b in range(batch)]
-    im = [out[width:, b * width : (b + 1) * width] for b in range(batch)]
-    return re, im
+    form = 0 if conj else 1
+    half = [one_sided(tables, which, form, a, b) for a, b in zip(re, im)]
+    full = [one_sided(tables, which, form, a.T, b.T) for a, b in half]
+    return [a.T for a, _ in full], [b.T for _, b in full]
 
 
 def field_grads(tables, wave_ref, window_ref, measured, scales):
@@ -182,70 +179,66 @@
     lax.fori_loop(first_unit, last_unit, step, 0)
 
 
-def push_kernel(count_ref, row_ref, col_ref, own_hbm, seen_hbm, plan_ref, out_hbm, own_ref, buffer_ref, sem, seen_sem, *, room):
+def push_kernel(count_hbm, row_hbm, col_hbm, own_hbm, seen_hbm, plan_ref, push_ref, own_ref,
+                count_ref, row_ref, col_ref, sems, seen_sem, *, room):
     width = own_ref.shape[2]
     units, seen_units = width // UNIT, seen_hbm.shape[1]
-    load = pltpu.make_async_copy(own_hbm, own_ref, sem)
-    load.start()
+    small = [
+        pltpu.make_async_copy(count_hbm, count_ref, sems.at[1]),
+        pltpu.make_async_copy(row_hbm, row_ref, sems.at[2]),
+        pltpu.make_async_copy(col_hbm, col_ref, sems.at[3]),
+    ]
+    load = pltpu.make_async_copy(own_hbm, own_ref, sems.at[0])
+    for copy in small + [load]:
+        copy.start()
+    for copy in small:
+        copy.wait()
     make_plan(count_ref, row_ref, col_ref, plan_ref, width, room)
-    load.wait()
+
+    def seen(i):
+        slot = plan_ref[PUSHED, i]
+        start = plan_ref[AT_PUSH, slot] + units - plan_ref[ROW, slot] // UNIT
+        return pltpu.make_async_copy(seen_hbm.at[slot], push_ref.at[pl.ds(start, seen_units)], seen_sem.at[i])
+
+    def begin(i, carry):
+        seen(i).start()
+        return carry
 
     def step(i, carry):
         slot = plan_ref[PUSHED, i]
-        start, low = plan_ref[AT_PUSH, slot], plan_ref[ROW, slot] // UNIT
-        seen = pltpu.make_async_copy(
-            seen_hbm.at[slot], buffer_ref.at[pl.ds(start + units - low, seen_units)], seen_sem
-        )
-        seen.start()
-        pack(plan_ref, slot, own_ref, buffer_ref, start, low, units)
-        seen.wait()
+        pack(plan_ref, slot, own_ref, push_ref, plan_ref[AT_PUSH, slot], plan_ref[ROW, slot] // UNIT, units)
         return carry
 
+    def end(i, carry):
+        seen(i).wait()
+        return carry
+
+    lax.fori_loop(0, plan_ref[TOTALS, 0], begin, 0)
+    load.wait()
     lax.fori_loop(0, plan_ref[TOTALS, 0], step, 0)
-    store = pltpu.make_async_copy(buffer_ref, out_hbm, sem)
-    store.start()
-    store.wait()
-
-
-def pull_kernel(plan_ref, own_hbm, out_hbm, own_ref, buffer_ref, sem):
-    load = pltpu.make_async_copy(own_hbm, own_ref, sem)
-    load.start()
-    load.wait()
-
+    lax.fori_loop(0, plan_ref[TOTALS, 0], end, 0)
+
+
+def pull_kernel(plan_ref, own_ref, pull_ref):
     def step(i, carry):
         slot = plan_ref[KEPT, i]
-        pack(plan_ref, slot, own_ref, buffer_ref, plan_ref[AT_PULL, slot], 0, (plan_ref[ROW, slot] + UNIT - 1) // UNIT)
+        pack(plan_ref, slot, own_ref, pull_ref, plan_ref[AT_PULL, slot], 0, (plan_ref[ROW, slot] + UNIT - 1) // UNIT)
         return carry
 
     lax.fori_loop(0, plan_ref[TOTALS, 1], step, 0)
-    store = pltpu.make_async_copy(buffer_ref, out_hbm, sem)
-    store.start()
-    store.wait()
-
-
-def grad_kernel(plan_ref, loss_in_ref, probe_hbm, own_hbm, came_hbm, seen_hbm, tables_hbm, grad_in_hbm,
-                grad_hbm, back_hbm, loss_ref,
-                probe_ref, own_ref, came_ref, seen_ref, tables_ref, grad_ref, back_ref, wave_ref, window_ref, sems,
-                *, pushed):
+
+
+def grad_kernel(plan_ref, probe_ref, own_ref, came_ref, tables_ref, *refs, pushed):
+    if pushed:
+        grad_ref, back_ref, loss_ref, wave_ref, window_ref = refs
+    else:
+        loss_in_ref, seen_ref, _, grad_ref, back_ref, loss_ref, wave_ref, window_ref = refs
     slices, planes, width, columns = own_ref.shape
     units = width // UNIT
     seen_units = width // (UNIT * UNIT)
-    came = pl.ds(units, came_hbm.shape[0])
-    loads = [
-        pltpu.make_async_copy(probe_hbm, probe_ref, sems.at[0]),
-        pltpu.make_async_copy(own_hbm, own_ref, sems.at[1]),
-        pltpu.make_async_copy(came_hbm, came_ref.at[came], sems.at[2]),
-        pltpu.make_async_copy(tables_hbm, tables_ref, sems.at[3]),
-    ]
-    if not pushed:
-        loads.append(pltpu.make_async_copy(seen_hbm, seen_ref, sems.at[4]))
-        loads.append(pltpu.make_async_copy(grad_in_hbm, grad_ref, sems.at[5]))
-    for load in loads:
-        load.start()
+    last = came_ref.shape[0] - 1
     if pushed:
         grad_ref[...] = jnp.zeros_like(grad_ref)
-    for load in loads:
-        load.wait()
     row_iota = lax.broadcasted_iota(jnp.int32, (width, width), 0)
     lane_iota = lax.broadcasted_iota(jnp.int32, (width, width), 1)
     count = plan_ref[TOTALS, 0 if pushed else 1]
@@ -260,17 +253,17 @@
             row, shift, here, there = place(plan_ref, slot, width, columns)
             mine = row_iota < row if pushed else row_iota >= row
             first = lane_iota >= shift
-            low = row // UNIT
             if pushed:
-                start = units + plan_ref[AT_PUSH, slot] - low
-                seen = came_ref[pl.ds(start + units, seen_units)]
+                start = plan_ref[AT_PUSH, slot] - row // UNIT
+                seen = came_ref[pl.ds(jnp.minimum(start + units, last + 1 - seen_units), seen_units)]
                 measured.append(seen.reshape(width, width))
             else:
-                start = units + plan_ref[AT_PULL, slot]
+                start = plan_ref[AT_PULL, slot]
                 measured.append(seen_ref[slot])
+            at = [jnp.clip(start + u, 0, last) for u in range(units)]
             for l in range(slices):
                 for p in range(planes):
-                    theirs = came_ref[pl.ds(start, units), l * planes + p].reshape(width, width)
+                    theirs = jnp.concatenate([came_ref[i, l * planes + p] for i in at], axis=0)
                     ours = jnp.where(first, own_ref[l, p, :, here], own_ref[l, p, :, there])
                     window_ref[b, l, p] = jnp.where(mine, ours, theirs)
             for p in range(planes):
@@ -304,31 +297,13 @@
 
         return loss
 
-    loss_ref[0] = lax.fori_loop(0, (count + BATCH - 1) // BATCH, step, loss_in_ref[0])
-    stores = [
-        pltpu.make_async_copy(grad_ref, grad_hbm, sems.at[0]),
-        pltpu.make_async_copy(back_ref, back_hbm, sems.at[1]),
-    ]
-    for store in stores:
-        store.start()
-    for store in stores:
-        store.wait()
-
-
-def add_kernel(plan_ref, before_ref, grad_in_hbm, pushed_hbm, pulled_hbm, grad_hbm,
-               grad_ref, pushed_ref, pulled_ref, sems):
+    before = jnp.float32(0.0) if pushed else loss_in_ref[0]
+    loss_ref[0] = lax.fori_loop(0, (count + BATCH - 1) // BATCH, step, before)
+
+
+def add_kernel(plan_ref, before_ref, grad_in_ref, pushed_ref, pulled_ref, grad_hbm, grad_ref, sems):
     slices, planes, width, columns = grad_ref.shape
     units = width // UNIT
-    loads = [pltpu.make_async_copy(grad_in_hbm.at[l], grad_ref.at[l], sems.at[l]) for l in range(slices)]
-    stores = [pltpu.make_async_copy(grad_ref.at[l], grad_hbm.at[l], sems.at[slices + l]) for l in range(slices)]
-    others = [
-        pltpu.make_async_copy(pushed_hbm, pushed_ref, sems.at[2 * slices]),
-        pltpu.make_async_copy(pulled_hbm, pulled_ref, sems.at[2 * slices + 1]),
-    ]
-    for load in others + loads:
-        load.start()
-    for load in others:
-        load.wait()
     lane_iota = lax.broadcasted_iota(jnp.int32, (UNIT, width), 1)
     row_iota = lax.broadcasted_iota(jnp.int32, (UNIT, width), 0)
 
@@ -348,8 +323,9 @@
 
         lax.fori_loop(begin, end, unit, 0)
 
+    stores = [pltpu.make_async_copy(grad_ref.at[l], grad_hbm.at[l], sems.at[l]) for l in range(slices)]
     for l in range(slices):
-        loads[l].wait()
+        grad_ref[l] = grad_in_ref[l]
 
         def returned(i, carry, l=l):
             slot = plan_ref[PUSHED, i]
@@ -400,6 +376,7 @@
     seen = intensities.reshape(cap, seen_units, UNIT, UNIT, width)
     room = sizes(cap, width)
     smem = pl.BlockSpec(memory_space=pltpu.SMEM)
+    vmem = pl.BlockSpec(memory_space=pltpu.VMEM)
     hbm = pl.BlockSpec(memory_space=pl.ANY)
     f32 = jnp.float32
 
@@ -409,20 +386,27 @@
     def shape(dims, dtype=f32):
         return jax.ShapeDtypeStruct(dims, dtype)
 
-    params = pltpu.CompilerParams(vmem_limit_bytes=48 << 20)
+    def params(mib):
+        return pltpu.CompilerParams(vmem_limit_bytes=mib << 20)
+
+    def cost(us):
+        return pl.CostEstimate(flops=int(us * 1e9), bytes_accessed=int(us * 1e6), transcendentals=0)
+
     strip = object_slices.shape
-    plan, push = pl.pallas_call(
+    plan, push, own = pl.pallas_call(
         functools.partial(push_kernel, room=room),
-        out_shape=(shape((8, cap), jnp.int32), shape(packed(room[0]))),
-        in_specs=[smem] * 3 + [hbm] * 2,
-        out_specs=(smem, hbm),
+        out_shape=(shape((8, cap), jnp.int32), shape(packed(room[0])), shape(strip)),
+        in_specs=[hbm] * 5,
+        out_specs=(smem, vmem, vmem),
         scratch_shapes=[
-            pltpu.VMEM(strip, f32),
-            pltpu.VMEM(packed(room[0]), f32),
-            pltpu.SemaphoreType.DMA,
-            pltpu.SemaphoreType.DMA,
+            pltpu.SMEM(counts.shape, jnp.int32),
+            pltpu.SMEM(row_offset.shape, jnp.int32),
+            pltpu.SMEM(col_offset.shape, jnp.int32),
+            pltpu.SemaphoreType.DMA((4,)),
+            pltpu.SemaphoreType.DMA((cap,)),
         ],
-        compiler_params=params,
+        compiler_params=params(16),
+        cost_estimate=cost(4),
         name="pack_pushed",
     )(counts, row_offset, col_offset, object_slices, seen)
     pushed = shifted(push, "tile", 1)
@@ -430,57 +414,43 @@
     pull = pl.pallas_call(
         pull_kernel,
         out_shape=shape(packed(room[2])),
-        in_specs=[smem, hbm],
-        out_specs=hbm,
-        scratch_shapes=[
-            pltpu.VMEM(strip, f32),
-            pltpu.VMEM(packed(room[2]), f32),
-            pltpu.SemaphoreType.DMA,
-        ],
-        compiler_params=params,
+        in_specs=[smem, vmem],
+        out_specs=vmem,
+        compiler_params=params(16),
+        cost_estimate=cost(1),
         name="pack_pulled",
-    )(before, object_slices)
+    )(before, own)
     pulled = shifted(pull, "tile", -1)
 
-    def grads(plan, loss, came, grad, back, is_pushed):
+    def grads(plan, came, back, *kept):
         return pl.pallas_call(
-            functools.partial(grad_kernel, pushed=is_pushed),
+            functools.partial(grad_kernel, pushed=not kept),
             out_shape=(shape(strip), shape(packed(back)), shape((1,))),
-            in_specs=[smem, smem] + [hbm] * 6,
-            out_specs=(hbm, hbm, smem),
+            in_specs=[smem] + [vmem] * 4 + ([smem, vmem, vmem] if kept else []),
+            out_specs=(vmem, vmem, smem),
             scratch_shapes=[
-                pltpu.VMEM(probe_wave.shape, f32),
-                pltpu.VMEM(strip, f32),
-                pltpu.VMEM(packed(came.shape[0] + 2 * units), f32),
-                pltpu.VMEM(intensities.shape, f32),
-                pltpu.VMEM(tables.shape, tables.dtype),
-                pltpu.VMEM(strip, f32),
-                pltpu.VMEM(packed(back), f32),
                 pltpu.VMEM((BATCH, slices, planes, width, width), f32),
                 pltpu.VMEM((BATCH, slices, planes, width, width), f32),
-                pltpu.SemaphoreType.DMA((6,)),
             ],
-            compiler_params=params,
-            name="grads_pushed" if is_pushed else "grads_kept",
-        )(plan, loss, probe_wave, object_slices, came, intensities, tables, grad)
-
-    grad, back, loss = grads(before, jnp.zeros((1,), f32), pushed, object_slices, room[1], True)
+            input_output_aliases={7: 0} if kept else {},
+            compiler_params=params(24),
+            cost_estimate=cost(10),
+            name="grads_kept" if kept else "grads_pushed",
+        )(plan, probe_wave, own, came, tables, *kept)
+
+    grad, back, loss = grads(before, pushed, room[1])
     returned = shifted(back, "tile", -1)
-    grad, back, loss = grads(plan, loss, pulled, grad, room[2], False)
+    grad, back, loss = grads(plan, pulled, room[2], loss, intensities, grad)
     given = shifted(back, "tile", 1)
     misfit_total = total_of(loss, "tile")
     grad = pl.pallas_call(
         add_kernel,
         out_shape=shape(strip),
-        in_specs=[smem, smem] + [hbm] * 3,
+        in_specs=[smem, smem] + [vmem] * 3,
         out_specs=hbm,
-        scratch_shapes=[
-            pltpu.VMEM(strip, f32),
-            pltpu.VMEM(packed(room[1]), f32),
-            pltpu.VMEM(packed(room[2]), f32),
-            pltpu.SemaphoreType.DMA((2 * slices + 2,)),
-        ],
-        compiler_params=params,
+        scratch_shapes=[pltpu.VMEM(strip, f32), pltpu.SemaphoreType.DMA((slices,))],
+        compiler_params=params(16),
+        cost_estimate=cost(4),
         name="add_returned",
     )(plan, before, grad, returned, given)
     return (grad, misfit_total)

time: 120 us -> 101 us (0.84)
  the two profiles are of different devices: /device:TPU:14 before, /device:TPU:0 now
where the time goes in v1:
time: 101 us; the launch traced here: 99.7 us
  waiting for transfers between devices  44.8 us (44%)
  starting transfers between devices  26 us (26%)
  Pallas kernels  17 us (17%)
  between operations  6.82 us (7%)
  local copies, waits for them, and re-layouts  5.14 us (5%)
    ppermute x5, waiting for transfers between devices, shifted(): return lax.ppermute(x, axis, [(i, (i + by) % peers) for i in range(peers)])  23.4 us
    ppermute x6, waiting for transfers between devices, other(): return lax.ppermute(x, axis, [(i, i ^ by) for i in range(peers)])  21.4 us
    ppermute x6, starting transfers between devices, other(): return lax.ppermute(x, axis, [(i, i ^ by) for i in range(peers)])  15.6 us
    ppermute x5, starting transfers between devices, shifted(): return lax.ppermute(x, axis, [(i, (i + by) % peers) for i in range(peers)])  10.4 us
    pallas_call x2, Pallas kernels, grads(): pl.pallas_call(functools.partial(grad_kernel, pushed=not kept), out_shape...  10.1 us
    unnamed x14, local copies, waits for them, and re-layouts  5.14 us
    pallas_call x1, Pallas kernels, local(): pl.pallas_call(add_kernel, out_shape=shape(strip), in_specs=[smem, smem]...  3.67 us
    pallas_call x1, Pallas kernels, local(): pl.pallas_call(functools.partial(push_kernel, room=room), out_shape=(shap...  2.59 us
  transfers between devices with their start and end apart: 11, of which 5 were waited for; matrix products, arithmetic and copies ran while one was open for 0% of the time, Pallas kernels for 9%

profile of v1, /device:TPU:0, one launch (start us, length us, event | category | flops | bytes accessed | tf_op | source)
XLA Modules:
  0.0 99.7 jit_solution(1174695497132351211)
XLA Ops:
  1.3 2.2 %copy-done = f32[4,2,128,1024]{3,2,1,0:T(8,128)S(1)} copy-done((f32[4,2,128,1024]{3,2,1,0:T(8,128)S(1)}, f32[4,2,128,1024]{3,2,1,0:T(8,128)}, u32[]{:S(2)}) %copy-start) | copy-done | bytes 4194328
  3.5 1.0 %copy-done.1 = f32[8,128,128]{2,1,0:T(8,128)S(1)} copy-done((f32[8,128,128]{2,1,0:T(8,128)S(1)}, f32[8,128,128]{2,1,0:T(8,128)}, u32[]{:S(2)}) %copy-start.1) | copy-done | bytes 524312
  4.5 0.7 copy-done.4
  5.2 0.7 copy-done.5
  5.8 2.6 %pack_pushed.1 = (s32[8,8]{1,0:T(8,128)S(1)}, f32[40,8,8,128]{3,2,1,0:T(8,128)S(1)}, f32[4,2,128,1024]{3,2,1,0:T(8,128)S(1)}) custom-call(s32[1]{0:T(128)S(6)} %copy.11.count_hbm, s32[8]{0:T(128)S(1)} %copy-done.4, s32[8]{0:T(128)S(1)} %copy-done.5, f32[4,2,128,1024]{3,2,1,0:T(8,128)S(1)} %copy-done, f32[8,2,8,8,128]{4,3,2,1,0:T(8,128)S(1)} %bitcast.1), custom_call_target="tpu_custom_call" | custom-call | flops 4000000000 | bytes 4000000 | tf_op jit(solution)/shard_map/pack_pushed/pallas_call | solution.py:396
  8.4 0.5 collective-permute-start.2
  9.0 2.7 %collective-permute-start = (s32[8,8]{1,0:T(8,128)S(1)}, s32[8,8]{1,0:T(8,128)S(1)}, u32[]{:S(2)}, u32[]{:S(2)}) collective-permute-start(s32[8,8]{1,0:T(8,128)S(1)} %get-tuple-element.11.plan_ref), channel_id=1, source_target_pairs={{0,1},{1,2},{2,3},{3,4},{4,5},{5,6},{6,7},{7,8},{8,9},{9,10},{10,1... | collective-permute-start | bytes 776 | tf_op jit(solution)/shard_map/ppermute | solution.py:350
  11.6 17.0 %collective-permute-done.plan_ref.before_ref = s32[8,8]{1,0:T(8,128)S(1)} collective-permute-done((s32[8,8]{1,0:T(8,128)S(1)}, s32[8,8]{1,0:T(8,128)S(1)}, u32[]{:S(2)}, u32[]{:S(2)}) %collective-permute-start) | collective-permute-done | bytes 288 | tf_op jit(solution)/shard_map/ppermute | solution.py:350
  28.6 0.6 pack_pulled.1
  29.3 0.0 copy-start.2
  29.3 0.1 collective-permute-start.1
  29.3 0.0 collective-permute-done.2.came_ref
  29.4 0.2 copy-done.3
  29.5 0.4 copy-done.6
  29.9 8.1 %grads_pushed.1 = (f32[4,2,128,1024]{3,2,1,0:T(8,128)S(1)}, f32[32,8,8,128]{3,2,1,0:T(8,128)S(1)}, f32[1]{0:T(128)}) custom-call(s32[8,8]{1,0:T(8,128)S(1)} %collective-permute-done.plan_ref.before_ref, f32[2,128,128]{2,1,0:T(8,128)S(1)} %copy-done.3, f32[4,2,128,1024]{3,2,1,0:T(8,128)S(1)} %get-tuple-element.12.own_ref, ...), custom_call_target="tpu_custom_call" | custom-call | flops 10000000000 | bytes 10000000 | tf_op jit(solution)/shard_map/grads_pushed/pallas_call | solution.py:426
  38.1 6.4 %collective-permute-done.1.came_ref = f32[40,8,8,128]{3,2,1,0:T(8,128)S(1)} collective-permute-done((f32[40,8,8,128]{3,2,1,0:T(8,128)S(1)}, f32[40,8,8,128]{3,2,1,0:T(8,128)S(1)}, u32[]{:S(2)}, u32[]{:S(2)}) %collective-permute-start.1) | collective-permute-done | bytes 1310752 | tf_op jit(solution)/shard_map/ppermute | solution.py:350
  44.5 2.0 %grads_kept.1 = (f32[4,2,128,1024]{3,2,1,0:T(8,128)S(1)}, f32[40,8,8,128]{3,2,1,0:T(8,128)S(1)}, f32[1]{0:T(128)}) custom-call(s32[8,8]{1,0:T(8,128)S(1)} %get-tuple-element.11.plan_ref, f32[2,128,128]{2,1,0:T(8,128)S(1)} %copy-done.3, f32[4,2,128,1024]{3,2,1,0:T(8,128)S(1)} %get-tuple-element.12.own_ref, ...), custom_call_target="tpu_custom_call", output_to_operand_aliasing={{0}: (7, {})} | custom-call | flops 10000000000 | bytes 10000000 | tf_op jit(solution)/shard_map/grads_kept/pallas_call | solution.py:426
  46.4 7.1 %collective-permute-start.4 = (f32[40,8,8,128]{3,2,1,0:T(8,128)S(1)}, f32[40,8,8,128]{3,2,1,0:T(8,128)S(1)}, u32[]{:S(2)}, u32[]{:S(2)}) collective-permute-start(f32[40,8,8,128]{3,2,1,0:T(8,128)S(1)} %get-tuple-element.18), channel_id=1, source_target_pairs={{0,1},{1,2},{2,3},{3,4},{4,5},{5,6},{6,7},{7,8},{8,9},{9,10},{10,1... | collective-permute-start | bytes 3932168 | tf_op jit(solution)/shard_map/ppermute | solution.py:350
  53.6 0.0 collective-permute-start.3
  53.6 2.9 %collective-permute-start.7 = (f32[1]{0:T(128)}, f32[1]{0:T(128)}, u32[]{:S(2)}, u32[]{:S(2)}) collective-permute-start(f32[1]{0:T(128)} %get-tuple-element.19), channel_id=1, source_target_pairs={{0,3},{1,2},{2,1},{3,0},{4,7},{5,6},{6,5},{7,4},{8,11},{9,10},{10,... | collective-permute-start | bytes 20 | tf_op jit(solution)/shard_map/ppermute | solution.py:358
  56.5 0.0 collective-permute-start.6
  56.5 0.1 collective-permute-start.5
  56.6 1.1 %collective-permute-done.5 = f32[1]{0:T(128)} collective-permute-done((f32[1]{0:T(128)}, f32[1]{0:T(128)}, u32[]{:S(2)}, u32[]{:S(2)}) %collective-permute-start.5) | collective-permute-done | bytes 36 | tf_op jit(solution)/shard_map/ppermute | solution.py:358
  59.0 0.0 collective-permute-done.7
  59.0 18.7 %collective-permute-done.6 = f32[1]{0:T(128)} collective-permute-done((f32[1]{0:T(128)}, f32[1]{0:T(128)}, u32[]{:S(2)}, u32[]{:S(2)}) %collective-permute-start.6) | collective-permute-done | bytes 36 | tf_op jit(solution)/shard_map/ppermute | solution.py:358
  78.9 9.4 %collective-permute-start.10 = (f32[1]{0:T(128)}, f32[1]{0:T(128)}, u32[]{:S(2)}, u32[]{:S(2)}) collective-permute-start(f32[1]{0:T(128)} %add.20), channel_id=1, source_target_pairs={{0,12},{1,13},{2,14},{3,15},{4,8},{5,9},{6,10},{7,11},{8,4},{9,5},... | collective-permute-start | bytes 20 | tf_op jit(solution)/shard_map/ppermute | solution.py:358
  88.3 1.3 %collective-permute-start.9 = (f32[1]{0:T(128)}, f32[1]{0:T(128)}, u32[]{:S(2)}, u32[]{:S(2)}) collective-permute-start(f32[1]{0:T(128)} %add.20), channel_id=1, source_target_pairs={{0,8},{1,9},{2,10},{3,11},{4,12},{5,13},{6,14},{7,15},{8,0},{9,1},... | collective-permute-start | bytes 20 | tf_op jit(solution)/shard_map/ppermute | solution.py:358
  89.6 1.9 %collective-permute-start.8 = (f32[1]{0:T(128)}, f32[1]{0:T(128)}, u32[]{:S(2)}, u32[]{:S(2)}) collective-permute-start(f32[1]{0:T(128)} %add.20), channel_id=1, source_target_pairs={{0,4},{1,5},{2,6},{3,7},{4,0},{5,1},{6,2},{7,3},{8,12},{9,13},{10,... | collective-permute-start | bytes 20 | tf_op jit(solution)/shard_map/ppermute | solution.py:358
  91.4 1.6 %collective-permute-done.8 = f32[1]{0:T(128)} collective-permute-done((f32[1]{0:T(128)}, f32[1]{0:T(128)}, u32[]{:S(2)}, u32[]{:S(2)}) %collective-permute-start.8) | collective-permute-done | bytes 36 | tf_op jit(solution)/shard_map/ppermute | solution.py:358
  94.9 0.0 collective-permute-done.3.pushed_ref
  94.9 0.0 collective-permute-done.4.pulled_ref
  94.9 3.7 %add_returned.1 = f32[4,2,128,1024]{3,2,1,0:T(8,128)} custom-call(s32[8,8]{1,0:T(8,128)S(1)} %get-tuple-element.11.plan_ref, s32[8,8]{1,0:T(8,128)S(1)} %collective-permute-done.plan_ref.before_ref, f32[4,2,128,1024]{3,2,1,0:T(8,128)S(1)} %get-tuple-element.16.grad_in_ref, f32[32,8,8,128]{3,2,1,0:T(8,128)S(1)} %collective-permute-done.3.pushed_ref, ...), custom_call_target="tpu_custom_call" | custom-call | flops 4000000000 | bytes 4000000 | tf_op jit(solution)/shard_map/add_returned/pallas_call | solution.py:446
  (9 shorter events, 0.0 us)
Async XLA Ops:
  1.3 2.2 %copy-start = (f32[4,2,128,1024]{3,2,1,0:T(8,128)S(1)}, f32[4,2,128,1024]{3,2,1,0:T(8,128)}, u32[]{:S(2)}) copy-start(f32[4,2,128,1024]{3,2,1,0:T(8,128)} %own_hbm.1) | copy-start | bytes 12582916
  3.5 1.0 %copy-start.1 = (f32[8,128,128]{2,1,0:T(8,128)S(1)}, f32[8,128,128]{2,1,0:T(8,128)}, u32[]{:S(2)}) copy-start(f32[8,128,128]{2,1,0:T(8,128)} %refs_1_.1) | copy-start | bytes 1572868
  4.5 0.7 copy-start.4
  5.2 0.7 copy-start.5
  8.4 20.9 %collective-permute-start.2 = (f32[40,8,8,128]{3,2,1,0:T(8,128)S(1)}, f32[40,8,8,128]{3,2,1,0:T(8,128)S(1)}, u32[]{:S(2)}, u32[]{:S(2)}) collective-permute-start(f32[40,8,8,128]{3,2,1,0:T(8,128)S(1)} %get-tuple-element.13), channel_id=1, source_target_pairs={{0,1},{1,2},{2,3},{3,4},{4,5},{5,6},{6,7},{7,8},{8,9},{9,10},{10,1... | collective-permute-start | bytes 3932168 | tf_op jit(solution)/shard_map/ppermute | solution.py:350
  9.0 19.7 %collective-permute-start = (s32[8,8]{1,0:T(8,128)S(1)}, s32[8,8]{1,0:T(8,128)S(1)}, u32[]{:S(2)}, u32[]{:S(2)}) collective-permute-start(s32[8,8]{1,0:T(8,128)S(1)} %get-tuple-element.11.plan_ref), channel_id=1, source_target_pairs={{0,1},{1,2},{2,3},{3,4},{4,5},{5,6},{6,7},{7,8},{8,9},{9,10},{10,1... | collective-permute-start | bytes 776 | tf_op jit(solution)/shard_map/ppermute | solution.py:350
  28.6 0.9 copy-start.3
  28.6 1.3 %copy-start.6 = (bf16[2,2,2,256,256]{4,3,2,1,0:T(8,128)(2,1)S(1)}, bf16[2,2,2,256,256]{4,3,2,1,0:T(8,128)(2,1)}, u32[]{:S(2)}) copy-start(bf16[2,2,2,256,256]{4,3,2,1,0:T(8,128)(2,1)} %constant.2.clone.tables_ref) | copy-start | bytes 3145732
  29.3 15.2 %copy-start.2 = (f32[8,128,128]{2,1,0:T(8,128)S(1)}, f32[8,128,128]{2,1,0:T(8,128)}, u32[]{:S(2)}) copy-start(f32[8,128,128]{2,1,0:T(8,128)} %refs_1_.1) | copy-start | bytes 1572868
  29.3 15.2 %collective-permute-start.1 = (f32[40,8,8,128]{3,2,1,0:T(8,128)S(1)}, f32[40,8,8,128]{3,2,1,0:T(8,128)S(1)}, u32[]{:S(2)}, u32[]{:S(2)}) collective-permute-start(f32[40,8,8,128]{3,2,1,0:T(8,128)S(1)} %pack_pulled.1), channel_id=1, source_target_pairs={{0,15},{1,0},{2,1},{3,2},{4,3},{5,4},{6,5},{7,6},{8,7},{9,8},{10,9... | collective-permute-start | bytes 3932168 | tf_op jit(solution)/shard_map/ppermute | solution.py:350
  46.4 48.5 %collective-permute-start.4 = (f32[40,8,8,128]{3,2,1,0:T(8,128)S(1)}, f32[40,8,8,128]{3,2,1,0:T(8,128)S(1)}, u32[]{:S(2)}, u32[]{:S(2)}) collective-permute-start(f32[40,8,8,128]{3,2,1,0:T(8,128)S(1)} %get-tuple-element.18), channel_id=1, source_target_pairs={{0,1},{1,2},{2,3},{3,4},{4,5},{5,6},{6,7},{7,8},{8,9},{9,10},{10,1... | collective-permute-start | bytes 3932168 | tf_op jit(solution)/shard_map/ppermute | solution.py:350
  53.6 41.3 %collective-permute-start.3 = (f32[32,8,8,128]{3,2,1,0:T(8,128)S(1)}, f32[32,8,8,128]{3,2,1,0:T(8,128)S(1)}, u32[]{:S(2)}, u32[]{:S(2)}) collective-permute-start(f32[32,8,8,128]{3,2,1,0:T(8,128)S(1)} %get-tuple-element.17), channel_id=1, source_target_pairs={{0,15},{1,0},{2,1},{3,2},{4,3},{5,4},{6,5},{7,6},{8,7},{9,8},{10,9... | collective-permute-start | bytes 3145736 | tf_op jit(solution)/shard_map/ppermute | solution.py:350
  53.6 5.4 %collective-permute-start.7 = (f32[1]{0:T(128)}, f32[1]{0:T(128)}, u32[]{:S(2)}, u32[]{:S(2)}) collective-permute-start(f32[1]{0:T(128)} %get-tuple-element.19), channel_id=1, source_target_pairs={{0,3},{1,2},{2,1},{3,0},{4,7},{5,6},{6,5},{7,4},{8,11},{9,10},{10,... | collective-permute-start | bytes 20 | tf_op jit(solution)/shard_map/ppermute | solution.py:358
  56.5 21.2 %collective-permute-start.6 = (f32[1]{0:T(128)}, f32[1]{0:T(128)}, u32[]{:S(2)}, u32[]{:S(2)}) collective-permute-start(f32[1]{0:T(128)} %get-tuple-element.19), channel_id=1, source_target_pairs={{0,2},{1,3},{2,0},{3,1},{4,6},{5,7},{6,4},{7,5},{8,10},{9,11},{10,... | collective-permute-start | bytes 20 | tf_op jit(solution)/shard_map/ppermute | solution.py:358
  56.5 1.2 %collective-permute-start.5 = (f32[1]{0:T(128)}, f32[1]{0:T(128)}, u32[]{:S(2)}, u32[]{:S(2)}) collective-permute-start(f32[1]{0:T(128)} %get-tuple-element.19), channel_id=1, source_target_pairs={{0,1},{1,0},{2,3},{3,2},{4,5},{5,4},{6,7},{7,6},{8,9},{9,8},{10,11... | collective-permute-start | bytes 20 | tf_op jit(solution)/shard_map/ppermute | solution.py:358
  78.9 14.8 %collective-permute-start.10 = (f32[1]{0:T(128)}, f32[1]{0:T(128)}, u32[]{:S(2)}, u32[]{:S(2)}) collective-permute-start(f32[1]{0:T(128)} %add.20), channel_id=1, source_target_pairs={{0,12},{1,13},{2,14},{3,15},{4,8},{5,9},{6,10},{7,11},{8,4},{9,5},... | collective-permute-start | bytes 20 | tf_op jit(solution)/shard_map/ppermute | solution.py:358
  88.3 5.4 %collective-permute-start.9 = (f32[1]{0:T(128)}, f32[1]{0:T(128)}, u32[]{:S(2)}, u32[]{:S(2)}) collective-permute-start(f32[1]{0:T(128)} %add.20), channel_id=1, source_target_pairs={{0,8},{1,9},{2,10},{3,11},{4,12},{5,13},{6,14},{7,15},{8,0},{9,1},... | collective-permute-start | bytes 20 | tf_op jit(solution)/shard_map/ppermute | solution.py:358
  89.6 3.5 %collective-permute-start.8 = (f32[1]{0:T(128)}, f32[1]{0:T(128)}, u32[]{:S(2)}, u32[]{:S(2)}) collective-permute-start(f32[1]{0:T(128)} %add.20), channel_id=1, source_target_pairs={{0,4},{1,5},{2,6},{3,7},{4,0},{5,1},{6,2},{7,3},{8,12},{9,13},{10,... | collective-permute-start | bytes 20 | tf_op jit(solution)/shard_map/ppermute | solution.py:358
